TPU v7x, 128 devices: a whole 4x4x4 slice. The times are simulated.
128 devices in a mesh: dp: 16 (over x, z_hi, core), tensor: 8 (over y, z_lo).
Axes of the slice: x: 4, y: 4, z: 4 (z_hi: 2, z_lo: 2; z = z_hi * 2 + z_lo), core: 2. Of those that a mesh axis runs over, the one named last changes fastest.
Arguments:
- inputs: bfloat16 [1024, 12288], P('tensor', 'dp'), may hold values from -11 to 14, as said below
- norm_gain: float32 [12288], P('dp'), may hold values from 0.5 to 1.5
- norm_bias: float32 [12288], P('dp'), may hold values from -3 to 3
- w_up: bfloat16 [12288, 24576], P('dp', 'tensor'), may hold values from -0.0546875 to 0.0546875
- b_up: float32 [24576], P('tensor'), may hold values from -3 to 3
- w_down: bfloat16 [24576, 12288], P('tensor', 'dp'), may hold values from -0.0390625 to 0.0390625
- b_down: float32 [12288], P('dp'), may hold values from -3 to 3
- d_branch: bfloat16 [1024, 12288], P('tensor', 'dp'), may hold values from -6 to 6
Outputs:
- branch: bfloat16 [1024, 12288], P('tensor', 'dp')
- grad_inputs: bfloat16 [1024, 12288], P('tensor', 'dp')
- grad_w_up: bfloat16 [12288, 24576], P('dp', 'tensor')
- grad_b_up: float32 [24576], P('tensor')
- grad_w_down: bfloat16 [24576, 12288], P('tensor', 'dp')
- grad_b_down: float32 [12288], P('dp')
- grad_gain: float32 [12288], P('dp')
- grad_bias: float32 [12288], P('dp')
Inputs may be any that keep to these rules, and one draw needn't show every extreme that they name: inputs are finite values of the residual stream.
All inputs are finite; a program needn't handle non-finite values.
Results may differ from a plain program's by a relative error of at most 0.025.
Values may be sent and summed in bfloat16 or wider, within the bound.
A program may use at most 128 MiB of HBM per device.

v0:
```python
import functools

import jax
import jax.numpy as jnp
from jax import lax
from jax.experimental import pallas as pl
from jax.experimental.pallas import tpu as pltpu
from jax.sharding import PartitionSpec as P

MESH = pl.DeviceIdType.MESH
F32, BF16 = jnp.float32, jnp.bfloat16

D = 12288
WIDE = 768
HALF = 1536
TOKENS = 1024
STRIP = 512
K0 = 0.7978845608028654
K1 = 0.044715

OWN = (16, 32, 32, 32, 16)
CHUNKS = len(OWN)
OFF = tuple(sum(OWN[:c]) for c in range(CHUNKS))
Z_FIRST = (2,)
T_PAIRS = (1, 2, 3, 4)
R_PAIRS = (0, 1, 2)
Z_ROWS = tuple((4 if c in Z_FIRST else 1) * OWN[c] for c in range(CHUNKS))
Z_OFF = tuple(sum(Z_ROWS[:c]) for c in range(CHUNKS))

ORDER = (
    ("TZ", 0, 1), ("TZ", 0, 3), ("TY", 0, 0), ("ST", 0, 0), ("TY", 0, 1), ("TY", 0, 3), ("NM", 0, 0), ("TZ", 0, 2),
    ("TZ", 0, 4), ("M", 0, 0), ("TY", 1, 0), ("TZ", 1, 1), ("A", 0, 0), ("M", 0, 1), ("TZ", 1, 2), ("TZ", 1, 3),
    ("TY", 0, 2), ("B", 0, 0), ("TY", 0, 4), ("A", 0, 1), ("M", 0, 3), ("M", 1, 0), ("A", 0, 3), ("C", 0, 0),
    ("A", 1, 0), ("TY", 1, 1), ("TY", 1, 2), ("B", 0, 1), ("M", 0, 2), ("M", 0, 4), ("B", 0, 3), ("TZ", 1, 4),
    ("A", 0, 2), ("A", 0, 4), ("TY", 1, 4), ("B", 1, 0), ("M", 1, 1), ("TY", 1, 3), ("A", 1, 1), ("M", 1, 2),
    ("C", 0, 1), ("B", 0, 4), ("M", 1, 4), ("C", 1, 0), ("B", 0, 2), ("B", 1, 1), ("A", 1, 2), ("M", 1, 3),
    ("A", 1, 3), ("A", 1, 4), ("G", 0, 0), ("C", 0, 2), ("C", 1, 1), ("B", 1, 3), ("E1", 0, 0), ("B", 1, 4),
    ("B", 1, 2), ("G", 0, 1), ("E2", 0, 0), ("C", 0, 3), ("E1", 1, 0), ("C", 1, 3), ("C", 1, 2), ("E1", 0, 1),
    ("E1", 1, 1), ("E3", 0, 0), ("G", 0, 3), ("G", 0, 2), ("C", 0, 4), ("E2", 0, 1), ("C", 1, 4), ("E1", 1, 2),
    ("E2", 1, 1), ("G", 0, 4), ("E2", 1, 0), ("E3", 0, 1), ("E1", 0, 2), ("E2", 1, 2), ("E1", 1, 3), ("F", 0, 0),
    ("F", 0, 1), ("E1", 1, 4), ("E3", 1, 1), ("E2", 0, 2), ("E3", 1, 0), ("F", 1, 1), ("E1", 0, 4), ("F", 1, 0),
    ("E2", 1, 3), ("E1", 0, 3), ("E3", 1, 2), ("H1", 0, 0), ("H1", 0, 1), ("F", 1, 2), ("E3", 1, 3), ("H1", 1, 1),
    ("E2", 1, 4), ("E2", 0, 4), ("F", 1, 3), ("E2", 0, 3), ("H1", 1, 0), ("E3", 1, 4), ("H", 0, 0), ("E3", 0, 2),
    ("E3", 0, 4), ("F", 1, 4), ("F", 0, 4), ("E3", 0, 3), ("F", 0, 2), ("H1", 1, 2), ("H", 1, 1), ("H", 1, 3),
    ("F", 0, 3), ("H", 1, 4), ("WD", 0, 1), ("H", 1, 2), ("H", 1, 0), ("S", 0, 0), ("H", 0, 4), ("H1", 0, 2),
    ("WD", 0, 0), ("Z", 0, 0), ("H", 0, 2), ("H", 0, 1), ("H", 0, 3),
)


def transposed_dot(left, right):
    return lax.dot_general(left, right, (((1,), (1,)), ((), ())), preferred_element_type=F32)


def dot_transposed(left, right):
    return lax.dot_general(left, right, (((0,), (0,)), ((), ())), preferred_element_type=F32)


def columns_to_rows(first, second):
    lane = lax.broadcasted_iota(jnp.int32, (128, 128), 1)
    return jnp.where(lane == 0, first, jnp.where(lane == 1, second, 0.0)).T[0:8, :]


def rows_to_columns(first, second):
    row = lax.broadcasted_iota(jnp.int32, (128, 128), 0)
    both = jnp.where(row == 0, first, jnp.where(row == 1, second, 0.0)).T
    return both[:, 0:1], both[:, 1:2]


def column_sums(load, width):
    def block(i, total):
        return total + load(pl.ds(pl.multiple_of(i * 16, 16), 16)).astype(F32)

    return jnp.sum(lax.fori_loop(0, TOKENS // 16, block, jnp.zeros((16, width), F32)), axis=0)


def kernel(
    x_ref, gain_ref, bias_ref, b_up_ref, b_down_ref, d_ref, w_up_hbm, w_down_hbm,
    branch_ref, grad_in_ref, grad_gain_ref, grad_bias_ref, grad_b_down_ref, gw_down_hbm, gh_hbm, nrm_hbm,
    w_up, w_down, dbr, nrm, part, core_in, x1_in, x2_in, z_in, full, t_out, t_in, t_acc,
    standard, grad_normed, inverse_ref, stats, back_stats, gb,
    load_sem, store_sem, t_send, t_recv, tz_send, tz_recv, core_send, core_recv, x1_send, x1_recv, x2_send, x2_recv,
    z_send, z_recv, ga_send, ga_recv, gx_send, gx_recv, gf_send, gf_recv, gc_send, gc_recv,
    ts_send, ts_recv, tr_send, tr_recv, st_send, st_recv, bs_send, bs_recv, gb_send, gb_recv,
):
    dp, tensor = lax.axis_index("dp"), lax.axis_index("tensor")
    xi, zh, core = dp // 4, (dp // 2) % 2, dp % 2
    yi, zl = tensor // 2, tensor % 2
    x_right, x_left, x_far = (xi + 1) % 4, (xi + 3) % 4, (xi + 2) % 4
    right = (x_right * 4 + zh * 2 + core, tensor)
    left = (x_left * 4 + zh * 2 + core, tensor)
    across = (xi * 4 + (1 - zh) * 2 + core, tensor)
    sibling = (xi * 4 + zh * 2 + (1 - core), tensor)
    t_pair = (dp, yi * 2 + (1 - zl))
    y_to = [(dp, ((yi + dy) % 4) * 2 + zl) for dy in (1, 2, 3)]
    t_to = y_to + [t_pair] + [(dp, ((yi + dy) % 4) * 2 + (1 - zl)) for dy in (1, 2, 3)]
    d_to = []
    for dx in range(4):
        for mz in range(2):
            for mc in range(2):
                if dx or mz or mc:
                    d_to.append((((xi + dx) % 4) * 4 + (1 - zh if mz else zh) * 2 + (1 - core if mc else core), tensor))

    loads = [[pltpu.make_async_copy(w_down_hbm, w_down, load_sem.at[0])]]
    loads.append([pltpu.make_async_copy(w_up_hbm.at[:, pl.ds(h * HALF, HALF)], w_up.at[h], load_sem.at[1 + h]) for h in range(2)])
    for copy in loads[0] + loads[1]:
        copy.start()

    barrier = pltpu.get_barrier_semaphore()
    for device in t_to + d_to:
        pl.semaphore_signal(barrier, inc=1, device_id=device, device_id_type=MESH)

    def rows_at(at, count):
        return pl.ds(pl.multiple_of(at, 16), count)

    for c in range(CHUNKS):
        dbr[rows_at(8 * OFF[c] + tensor * OWN[c], OWN[c]), :] = d_ref[OFF[c] : OFF[c] + OWN[c], :]
    pl.semaphore_wait(barrier, len(t_to) + len(d_to))

    sent = []

    def send(source, target, sends, receives, index, device):
        copy = pltpu.make_async_remote_copy(
            src_ref=source, dst_ref=target, send_sem=sends.at[index], recv_sem=receives.at[index],
            device_id=device, device_id_type=MESH,
        )
        copy.start()
        sent.append(copy)
        return copy

    stores = []

    def store(source, target):
        copy = pltpu.make_async_copy(source, target, store_sem.at[len(stores)])
        copy.start()
        stores.append(copy)

    pair_in, token_in, core_arrives, x1_arrives, x2_arrives, z_arrives = {}, {}, {}, {}, {}, {}
    own_in, neighbour_in, far_in, core_full, branch_in, half_in = {}, {}, {}, {}, {}, {}
    small = {}
    tokens = (dbr, nrm)

    def pair_tokens(k, c):
        place = tokens[k].at[rows_at(8 * OFF[c] + tensor * OWN[c], OWN[c])]
        pair_in[k, c] = send(place, place, tz_send, tz_recv, (k, c), t_pair)

    def gather_tokens(k, c):
        if c in T_PAIRS:
            pair_in[k, c].wait_recv()
            place = tokens[k].at[rows_at(8 * OFF[c] + yi * 2 * OWN[c], 2 * OWN[c])]
            to = y_to
        else:
            place = tokens[k].at[rows_at(8 * OFF[c] + tensor * OWN[c], OWN[c])]
            to = t_to
        token_in[k, c] = [send(place, place, t_send, t_recv, (k, c, s), device) for s, device in enumerate(to)]

    def statistics(k, c):
        widened = x_ref[...].astype(F32)
        total = jnp.sum(widened, axis=1, keepdims=True)
        off = widened - total / WIDE
        stats[0] = columns_to_rows(total, jnp.sum(off * off, axis=1, keepdims=True))
        small["forward"] = [send(stats.at[0], stats.at[s + 1], st_send, st_recv, s, device) for s, device in enumerate(d_to)]

    def normalise(k, c):
        for copy in small["forward"]:
            copy.wait_recv()
        sums = [stats[s, 0:1, :] for s in range(16)]
        mean = functools.reduce(jnp.add, sums) / D
        spread = jnp.zeros_like(mean)
        for s in range(16):
            apart = sums[s] / WIDE - mean
            spread = spread + (stats[s, 1:2, :] + WIDE * (apart * apart))
        mean, inverse = rows_to_columns(mean, lax.rsqrt(spread / D + 1e-05))
        inverse_ref[...] = jnp.broadcast_to(inverse, (128, 128))
        gain, bias = gain_ref[...].reshape(1, WIDE), bias_ref[...].reshape(1, WIDE)
        for c in range(CHUNKS):
            rows = slice(OFF[c], OFF[c] + OWN[c])
            std = (x_ref[rows, :].astype(F32) - mean[rows]) * inverse[rows]
            standard[rows, :] = std
            nrm[rows_at(8 * OFF[c] + tensor * OWN[c], OWN[c]), :] = (std * gain + bias).astype(BF16)

    def accumulate(k, c, start, count, others):
        size = 32 if count % 32 == 0 else 16

        def block(i, _):
            at = i * size
            rows = rows_at(8 * OFF[c] + start + at, size)
            value = part[k, core, rows, :].astype(F32)
            for load in others:
                value = value + load(at, size).astype(F32)
            part[k, core, rows, :] = value.astype(BF16)
            return 0

        if count == size:
            block(0, 0)
        else:
            lax.fori_loop(0, count // size, block, 0)

    def multiply(k, c):
        if (k, c) == (k, 0):
            for copy in loads[k]:
                copy.wait()
        for copy in token_in[k, c]:
            copy.wait_recv()
        rows = pl.ds(8 * OFF[c], 8 * OWN[c])
        core_arrives[k, c] = pltpu.make_async_remote_copy(
            src_ref=part.at[k, 1 - core, rows], dst_ref=core_in.at[k, rows], send_sem=core_send.at[k, c],
            recv_sem=core_recv.at[k, c], device_id=sibling, device_id_type=MESH,
        )
        sent.append(core_arrives[k, c])

        def one(step, _):
            half = (1 - core) * (1 - step) + core * step
            if k:
                value = jnp.dot(nrm[rows, :], w_up[half], preferred_element_type=F32)
            else:
                value = transposed_dot(dbr[rows, :], w_down[half])
            part[k, half, rows, :] = value.astype(BF16)

            @pl.when(step == 0)
            def _():
                core_arrives[k, c].start()

            return 0

        lax.fori_loop(0, 2, one, 0)

    def part_rows(k, c, start, count):
        return part.at[k, core, rows_at(8 * OFF[c] + start, count)]

    def add_core(k, c):
        p = OWN[c]
        core_arrives[k, c].wait_recv()

        def add(start, count):
            accumulate(k, c, start, count, [lambda at, size: core_in[k, rows_at(8 * OFF[c] + start + at, size), :]])

        if c in Z_FIRST:
            add((1 - zh) * 4 * p, 4 * p)
            z_arrives[k, c] = send(
                part_rows(k, c, (1 - zh) * 4 * p, 4 * p), z_in.at[k, pl.ds(Z_OFF[c], 4 * p)], z_send, z_recv, (k, c), across
            )
            add(zh * 4 * p, 4 * p)
        else:
            add(x_far * 2 * p, 2 * p)
            x1_arrives[k, c] = [
                send(
                    part_rows(k, c, x_far * 2 * p + side * p, p), x1_in.at[k, side, pl.ds(OFF[c], p)],
                    x1_send, x1_recv, (k, c, side), device,
                )
                for side, device in enumerate((right, left))
            ]
            for piece in (x_right, x_left, xi):
                add(piece * 2 * p, 2 * p)

    def add_first(k, c):
        p = OWN[c]
        if c in Z_FIRST:
            z_arrives[k, c].wait_recv()

            def add(piece):
                start = piece * p
                accumulate(
                    k, c, zh * 4 * p + start, p, [lambda at, size: z_in[k, rows_at(Z_OFF[c] + start + at, size), :]]
                )

            add(x_far)
            x1_arrives[k, c] = [
                send(
                    part_rows(k, c, zh * 4 * p + x_far * p + side * (p // 2), p // 2),
                    x1_in.at[k, side, pl.ds(OFF[c], p // 2)], x1_send, x1_recv, (k, c, side), device,
                )
                for side, device in enumerate((right, left))
            ]
            for piece in (x_right, x_left, xi):
                add(piece)
        else:
            add_x1(k, c, 2 * p, 0)

    def add_x1(k, c, size, base):
        x2_arrives[k, c] = []
        for side, (piece, device) in enumerate(((x_right, right), (x_left, left))):
            x1_arrives[k, c][side].wait_recv()
            accumulate(
                k, c, base + piece * size + side * (size // 2), size // 2,
                [lambda at, count, side=side: x1_in[k, side, rows_at(OFF[c] + at, count), :]],
            )
            x2_arrives[k, c].append(
                send(
                    part_rows(k, c, base + piece * size, size), x2_in.at[k, side, pl.ds(2 * OFF[c], size)],
                    x2_send, x2_recv, (k, c, side), device,
                )
            )

    def add_second(k, c):
        p = OWN[c]
        if c in Z_FIRST:
            add_x1(k, c, p, zh * 4 * p)
            return
        for copy in x2_arrives[k, c]:
            copy.wait_recv()

        def add(sub):
            start = sub * p
            accumulate(
                k, c, xi * 2 * p + start, p,
                [lambda at, size, side=side: x2_in[k, side, rows_at(2 * OFF[c] + start + at, size), :] for side in range(2)],
            )

        add(1 - zh)
        z_arrives[k, c] = send(
            part_rows(k, c, xi * 2 * p + (1 - zh) * p, p), z_in.at[k, pl.ds(Z_OFF[c], p)], z_send, z_recv, (k, c), across
        )
        add(zh)

    def activate(_, c):
        p = OWN[c]
        if c in Z_FIRST:
            mine = zh * 4 * p + xi * p
            for k in range(2):
                for copy in x2_arrives[k, c]:
                    copy.wait_recv()
        else:
            mine = xi * 2 * p + zh * p
            for k in range(2):
                z_arrives[k, c].wait_recv()
        bias = b_up_ref[pl.ds(pl.multiple_of(core * HALF, HALF), HALF)].reshape(1, HALF)

        def total(k, at):
            value = part[k, core, rows_at(8 * OFF[c] + mine + at, 16), :].astype(F32)
            if c in Z_FIRST:
                for side in range(2):
                    value = value + x2_in[k, side, rows_at(2 * OFF[c] + at, 16), :].astype(F32)
                return value
            return value + z_in[k, rows_at(Z_OFF[c] + at, 16), :].astype(F32)

        def block(i, _):
            at = i * 16
            rows = rows_at(8 * OFF[c] + mine + at, 16)
            h = total(1, at) + bias
            square = h * h
            t = jnp.tanh(K0 * (h + K1 * (square * h)))
            full[0, core, rows, :] = (0.5 * h * (1.0 + t)).astype(BF16)
            slope = 0.5 * (1.0 + t) + 0.5 * h * (1.0 - t * t) * (K0 * (1.0 + 3.0 * K1 * square))
            full[1, core, rows, :] = (total(0, at) * slope).astype(BF16)
            return 0

        lax.fori_loop(0, p // 16, block, 0)
        for k in (1, 0):
            place = full.at[k, core, rows_at(8 * OFF[c] + mine, p)]
            to = (right, left) if c in Z_FIRST else (across,)
            own_in[k, c] = [send(place, place, ga_send, ga_recv, (k, c, s), device) for s, device in enumerate(to)]

    def full_rows(k, c, start, count):
        return full.at[k, core, rows_at(8 * OFF[c] + start, count)]

    def to_sibling(k, c, start, count):
        arrivals = core_full.setdefault((k, c), [])
        place = full_rows(k, c, start, count)
        arrivals.append(send(place, place, gc_send, gc_recv, (k, c, len(arrivals)), sibling))

    def forward(k, c, arrivals, size, base):
        made = []
        for side, (piece, device) in enumerate(((x_left, right), (x_right, left))):
            arrivals[side].wait_recv()
            place = full_rows(k, c, base + piece * size + side * (size // 2), size // 2)
            made.append(send(place, place, gf_send, gf_recv, (k, c, side), device))
        return made

    def gather_first(k, c):
        p = OWN[c]
        if c in Z_FIRST:
            far_in[k, c] = forward(k, c, own_in[k, c], p, zh * 4 * p)
        else:
            own_in[k, c][0].wait_recv()
            place = full_rows(k, c, xi * 2 * p, 2 * p)
            neighbour_in[k, c] = [
                send(place, place, gx_send, gx_recv, (k, c, side), device) for side, device in enumerate((right, left))
            ]
            to_sibling(k, c, xi * 2 * p, 2 * p)

    def gather_second(k, c):
        p = OWN[c]
        if c in Z_FIRST:
            for copy in far_in[k, c]:
                copy.wait_recv()
            place = full_rows(k, c, zh * 4 * p, 4 * p)
            neighbour_in[k, c] = [send(place, place, gx_send, gx_recv, (k, c, 0), across)]
            to_sibling(k, c, zh * 4 * p, 4 * p)
        else:
            far_in[k, c] = forward(k, c, neighbour_in[k, c], 2 * p, 0)
            for piece in (x_left, x_right):
                to_sibling(k, c, piece * 2 * p, 2 * p)

    def gather_third(k, c):
        p = OWN[c]
        if c in Z_FIRST:
            neighbour_in[k, c][0].wait_recv()
            to_sibling(k, c, (1 - zh) * 4 * p, 4 * p)
        else:
            for copy in far_in[k, c]:
                copy.wait_recv()
            to_sibling(k, c, x_far * 2 * p, 2 * p)

    def multiply_back(k, c):
        p = OWN[c]
        for copy in core_full[k, c]:
            copy.wait_recv()
        rows = pl.ds(8 * OFF[c], 8 * p)

        def tile(j, _):
            at = pl.ds(pl.multiple_of(j * 256, 256), 256)
            if k:
                value = transposed_dot(full[1, 0, rows, :], w_up[0, at, :])
                value += transposed_dot(full[1, 1, rows, :], w_up[1, at, :])
            else:
                value = jnp.dot(full[0, 0, rows, :], w_down[0, :, at], preferred_element_type=F32)
                value += jnp.dot(full[0, 1, rows, :], w_down[1, :, at], preferred_element_type=F32)
            t_out[k, rows, at] = value.astype(BF16)
            return 0

        lax.fori_loop(0, WIDE // 256, tile, 0)
        if k:
            for half in range(2):
                store(full.at[1, half, rows], gh_hbm.at[rows, pl.ds(half * HALF, HALF)])
            store(nrm.at[rows], nrm_hbm.at[rows])
        branch_in[k, c] = []
        if c in R_PAIRS:
            for s, device in enumerate(y_to):
                place = t_out.at[k, rows_at(8 * OFF[c] + (device[1] // 2) * 2 * p, 2 * p)]
                target = t_in.at[k, pl.ds(7 * OFF[c] + s * 2 * p, 2 * p)]
                branch_in[k, c].append(send(place, target, ts_send, ts_recv, (k, c, s), device))
        else:
            for s, device in enumerate(t_to):
                place = t_out.at[k, rows_at(8 * OFF[c] + device[1] * p, p)]
                target = t_in.at[k, pl.ds(7 * OFF[c] + s * p, p)]
                branch_in[k, c].append(send(place, target, ts_send, ts_recv, (k, c, s), device))

    def halve_tokens(k, c):
        p = OWN[c]
        for copy in branch_in[k, c]:
            copy.wait_recv()

        def total(sub):
            value = t_out[k, rows_at(8 * OFF[c] + (yi * 2 + sub) * p, p), :].astype(F32)
            for s in range(3):
                value = value + t_in[k, rows_at(7 * OFF[c] + s * 2 * p + sub * p, p), :].astype(F32)
            return value

        place = rows_at(8 * OFF[c] + (yi * 2 + 1 - zl) * p, p)
        t_out[k, place, :] = total(1 - zl).astype(BF16)
        half_in[k, c] = send(
            t_out.at[k, place], t_in.at[k, pl.ds(7 * OFF[c] + 6 * p, p)], tr_send, tr_recv, (k, c), t_pair
        )
        t_acc[k, OFF[c] : OFF[c] + p, :] = total(zl)

    def finish_tokens(k, c):
        p = OWN[c]
        rows = slice(OFF[c], OFF[c] + p)
        if c in R_PAIRS:
            half_in[k, c].wait_recv()
            value = t_acc[k, rows, :] + t_in[k, 7 * OFF[c] + 6 * p : 7 * OFF[c] + 7 * p, :].astype(F32)
        else:
            for copy in branch_in[k, c]:
                copy.wait_recv()
            value = t_out[k, rows_at(8 * OFF[c] + tensor * p, p), :].astype(F32)
            for s in range(7):
                value = value + t_in[k, 7 * OFF[c] + s * p : 7 * OFF[c] + (s + 1) * p, :].astype(F32)
        if k:
            grad_normed[rows, :] = value
        else:
            branch_ref[rows, :] = (value + b_down_ref[...].reshape(1, WIDE)).astype(BF16)

    def weight_down(_, half):
        def strip(i, _):
            at = pl.ds(pl.multiple_of(i * STRIP, STRIP), STRIP)
            w_down[half, at, :] = dot_transposed(full[0, half, :, at], dbr[...]).astype(BF16)
            return 0

        lax.fori_loop(0, HALF // STRIP, strip, 0)
        store(w_down.at[half], gw_down_hbm.at[pl.ds(half * HALF, HALF)])
        if half == 0:
            grad_b_down_ref[...] = column_sums(lambda rows: dbr[rows, :], WIDE)

    def back_sums(k, c):
        gn, std = grad_normed[...], standard[...]
        scaled = gn * gain_ref[...].reshape(1, WIDE)
        back_stats[0] = columns_to_rows(
            jnp.sum(scaled, axis=1, keepdims=True), jnp.sum(scaled * std, axis=1, keepdims=True)
        )
        small["back"] = [
            send(back_stats.at[0], back_stats.at[s + 1], bs_send, bs_recv, s, device) for s, device in enumerate(d_to)
        ]
        gb[0, 0:1, :] = jnp.sum(gn * std, axis=0, keepdims=True)
        gb[0, 1:2, :] = jnp.sum(gn, axis=0, keepdims=True)
        gb[0, 2:8, :] = jnp.zeros((6, WIDE), F32)
        small["gains"] = [send(gb.at[0], gb.at[s + 1], gb_send, gb_recv, s, device) for s, device in enumerate(t_to)]

    def grad_inputs(k, c):
        for copy in small["back"]:
            copy.wait_recv()
        first = functools.reduce(jnp.add, [back_stats[s, 0:1, :] for s in range(16)]) / D
        second = functools.reduce(jnp.add, [back_stats[s, 1:2, :] for s in range(16)]) / D
        first, second = rows_to_columns(first, second)
        scaled = grad_normed[...] * gain_ref[...].reshape(1, WIDE)
        grad_in_ref[...] = (inverse_ref[:, 0:1] * (scaled - first - standard[...] * second)).astype(BF16)
        for copy in small["gains"]:
            copy.wait_recv()
        both = functools.reduce(jnp.add, [gb[s] for s in range(8)])
        grad_gain_ref[...] = both[0]
        grad_bias_ref[...] = both[1]

    steps = {
        "TZ": pair_tokens, "TY": gather_tokens, "ST": statistics, "NM": normalise, "M": multiply, "A": add_core,
        "B": add_first, "C": add_second, "G": activate, "E1": gather_first, "E2": gather_second, "E3": gather_third,
        "F": multiply_back, "H1": halve_tokens, "H": finish_tokens, "WD": weight_down,
        "S": back_sums, "Z": grad_inputs,
    }
    for name, k, c in ORDER:
        steps[name](k, c)
    for copy in stores:
        copy.wait()
    for copy in sent:
        copy.wait_send()


def last_kernel(
    nrm_hbm, gh_hbm, gw_down_hbm, branch_in, grad_in_in, gain_in, bias_in, b_down_in,
    branch_out, grad_in_out, gw_up_out, b_up_out, gw_down_out, b_down_out, gain_out, bias_out,
    nrm, gh, gw_up, gw_down, branch, grad_in, gain, bias, b_down, in_sem, out_sem,
):
    strips, parts = 2 * HALF // STRIP, 4

    def columns(i):
        return pl.ds(i * STRIP, STRIP)

    ins, outs = [], []

    def fetch(source, target):
        copy = pltpu.make_async_copy(source, target, in_sem.at[len(ins)])
        copy.start()
        ins.append(copy)
        return copy

    def put(source, target):
        copy = pltpu.make_async_copy(source, target, out_sem.at[len(outs)])
        copy.start()
        outs.append(copy)

    first = fetch(nrm_hbm, nrm)
    strip_in = [fetch(gh_hbm.at[:, columns(i)], gh.at[i]) for i in range(strips)]
    rows = [pl.ds(i * (2 * HALF // parts), 2 * HALF // parts) for i in range(parts)]
    passing = [(fetch(gw_down_hbm.at[r], gw_down.at[r]), gw_down.at[r], gw_down_out.at[r]) for r in rows]
    for source, held, target in (
        (branch_in, branch, branch_out), (grad_in_in, grad_in, grad_in_out), (gain_in, gain, gain_out),
        (bias_in, bias, bias_out), (b_down_in, b_down, b_down_out),
    ):
        passing.append((fetch(source, held), held, target))
    first.wait()
    for i in range(strips):
        strip_in[i].wait()
        b_up_out[i * STRIP : (i + 1) * STRIP] = column_sums(lambda r: gh[i, r, :], STRIP)
        gw_up[i] = dot_transposed(nrm[...], gh[i]).astype(BF16)
        put(gw_up.at[i], gw_up_out.at[:, columns(i)])
        if i >= 2:
            for copy, held, target in passing[(i - 2) * 3 : (i - 1) * 3]:
                copy.wait()
                put(held, target)
    for copy in outs:
        copy.wait()


def on_device(inputs, norm_gain, norm_bias, w_up, b_up, w_down, b_down, d_branch):
    vmem = pl.BlockSpec(memory_space=pltpu.VMEM)
    hbm = pl.BlockSpec(memory_space=pl.ANY)
    shape = jax.ShapeDtypeStruct

    def pair(*size):
        return [pltpu.SemaphoreType.DMA(size)] * 2

    branch, grad_in, grad_gain, grad_bias, grad_b_down, grad_w_down, gh, nrm = pl.pallas_call(
        kernel,
        out_shape=(
            shape((128, WIDE), BF16), shape((128, WIDE), BF16), shape((WIDE,), F32), shape((WIDE,), F32),
            shape((WIDE,), F32), shape((2 * HALF, WIDE), BF16), shape((TOKENS, 2 * HALF), BF16), shape((TOKENS, WIDE), BF16),
        ),
        in_specs=[vmem] * 6 + [hbm] * 2,
        out_specs=(vmem,) * 5 + (hbm,) * 3,
        scratch_shapes=[
            pltpu.VMEM((2, WIDE, HALF), BF16),
            pltpu.VMEM((2, HALF, WIDE), BF16),
            pltpu.VMEM((TOKENS, WIDE), BF16),
            pltpu.VMEM((TOKENS, WIDE), BF16),
            pltpu.VMEM((2, 2, TOKENS, HALF), BF16),
            pltpu.VMEM((2, TOKENS, HALF), BF16),
            pltpu.VMEM((2, 2, 128, HALF), BF16),
            pltpu.VMEM((2, 2, 256, HALF), BF16),
            pltpu.VMEM((2, sum(Z_ROWS), HALF), BF16),
            pltpu.VMEM((2, 2, TOKENS, HALF), BF16),
            pltpu.VMEM((2, TOKENS, WIDE), BF16),
            pltpu.VMEM((2, 7 * 128, WIDE), BF16),
            pltpu.VMEM((2, 128, WIDE), F32),
            pltpu.VMEM((128, WIDE), F32),
            pltpu.VMEM((128, WIDE), F32),
            pltpu.VMEM((128, 128), F32),
            pltpu.VMEM((16, 8, 128), F32),
            pltpu.VMEM((16, 8, 128), F32),
            pltpu.VMEM((8, 8, WIDE), F32),
            pltpu.SemaphoreType.DMA((3,)), pltpu.SemaphoreType.DMA((2 + 3 * CHUNKS,)),
            *pair(2, CHUNKS, 7),
            *pair(2, CHUNKS),
            *pair(2, CHUNKS),
            *pair(2, CHUNKS, 2),
            *pair(2, CHUNKS, 2),
            *pair(2, CHUNKS),
            *pair(2, CHUNKS, 2),
            *pair(2, CHUNKS, 2),
            *pair(2, CHUNKS, 2),
            *pair(2, CHUNKS, 4),
            *pair(2, CHUNKS, 7),
            *pair(2, CHUNKS),
            *pair(15), *pair(15), *pair(7),
        ],
        compiler_params=pltpu.CompilerParams(collective_id=0, has_side_effects=True, vmem_limit_bytes=63 * 2**20),
    )(inputs, norm_gain, norm_bias, b_up, b_down, d_branch, w_up, w_down.reshape(2, HALF, WIDE))
    return pl.pallas_call(
        last_kernel,
        out_shape=(
            shape((128, WIDE), BF16), shape((128, WIDE), BF16), shape((WIDE, 2 * HALF), BF16), shape((2 * HALF,), F32),
            shape((2 * HALF, WIDE), BF16), shape((WIDE,), F32), shape((WIDE,), F32), shape((WIDE,), F32),
        ),
        in_specs=[hbm] * 8,
        out_specs=(hbm, hbm, hbm, vmem, hbm, hbm, hbm, hbm),
        scratch_shapes=[
            pltpu.VMEM((TOKENS, WIDE), BF16),
            pltpu.VMEM((6, TOKENS, STRIP), BF16),
            pltpu.VMEM((6, WIDE, STRIP), BF16),
            pltpu.VMEM((2 * HALF, WIDE), BF16),
            pltpu.VMEM((128, WIDE), BF16), pltpu.VMEM((128, WIDE), BF16),
            pltpu.VMEM((WIDE,), F32), pltpu.VMEM((WIDE,), F32), pltpu.VMEM((WIDE,), F32),
            pltpu.SemaphoreType.DMA((16,)), pltpu.SemaphoreType.DMA((15,)),
        ],
        compiler_params=pltpu.CompilerParams(vmem_limit_bytes=63 * 2**20),
    )(nrm, gh, grad_w_down, branch, grad_in, grad_gain, grad_bias, grad_b_down)


def solution(mesh):
    placed = (
        P("tensor", "dp"), P("dp"), P("dp"), P("dp", "tensor"), P("tensor"), P("tensor", "dp"), P("dp"), P("tensor", "dp"),
    )
    return jax.shard_map(
        on_device,
        mesh=mesh,
        in_specs=placed,
        out_specs=(
            P("tensor", "dp"), P("tensor", "dp"), P("dp", "tensor"), P("tensor"), P("tensor", "dp"), P("dp"), P("dp"), P("dp"),
        ),
        check_vma=False,
    )
```

profile of v0, /device:TPU:1, one launch (start us, length us, event | category | flops | bytes accessed | tf_op | source)
XLA Modules:
  0.0 156.0 jit_solution(1217698535476921135)
XLA Ops:
  0.6 143.3 %shard_map.143 = (bf16[128,768]{1,0:T(8,128)(2,1)}, bf16[128,768]{1,0:T(8,128)(2,1)}, f32[768]{0:T(1024)}, f32[768]{0:T(1024)}, f32[768]{0:T(1024)}, /*index=5*/...) custom-call(bf16[128,768]{1,0:T(8,128)(2,1)} %x_ref.1, f32[768]{0:T(1024)} %gain_ref.1, ...), custom_call_target="tpu_custom_call" | custom-call | tf_op jit(solution)/shard_map/pallas_call | solution.py:580
  143.9 11.9 %shard_map.144 = (bf16[128,768]{1,0:T(8,128)(2,1)}, bf16[128,768]{1,0:T(8,128)(2,1)}, bf16[768,3072]{1,0:T(8,128)(2,1)}, f32[3072]{0:T(1024)}, bf16[3072,768]{1,...) custom-call(bf16[1024,768]{1,0:T(8,128)(2,1)} %get-tuple-element.16.nrm_hbm, ...), custom_call_target="tpu_custom_call" | custom-call | tf_op jit(solution)/shard_map/pallas_call | solution.py:625
where the time goes:
time: 156 us
  Pallas kernels  155 us (99%)
    pallas_call x1, Pallas kernels, on_device(): pl.pallas_call(kernel, out_shape=(shape((128, WIDE), BF16), shape((128, W...  143 us
    pallas_call x1, Pallas kernels, on_device(): pl.pallas_call(last_kernel, out_shape=(shape((128, WIDE), BF16), shape((1...  11.9 us

commit v1 on v0

v1 whole, which is shorter than its diff:
```python
import functools

import jax
import jax.numpy as jnp
from jax import lax
from jax.experimental import pallas as pl
from jax.experimental.pallas import tpu as pltpu
from jax.sharding import PartitionSpec as P

MESH = pl.DeviceIdType.MESH
F32, BF16 = jnp.float32, jnp.bfloat16

D = 12288
WIDE = 768
HALF = 1536
TOKENS = 1024
STRIP = 512
K0 = 0.7978845608028654
K1 = 0.044715

OWN = (32, 32, 32, 16, 16)
CHUNKS = len(OWN)
OFF = tuple(sum(OWN[:c]) for c in range(CHUNKS))
SUM_Z = ((0, 2), (0, 3), (1, 2))
GATHER_X = ((0, 0), (0, 3), (1, 3))
T_PAIRS = (1, 2, 3, 4)
R_PAIRS = (0,)
Z_ROWS = tuple(tuple((4 if (k, c) in SUM_Z else 1) * OWN[c] for c in range(CHUNKS)) for k in range(2))
Z_OFF = tuple(tuple(sum(rows[:c]) for c in range(CHUNKS)) for rows in Z_ROWS)

ORDER = (
    ("TZ", 0, 1), ("TY", 0, 0), ("TZ", 0, 3), ("TZ", 0, 2), ("TZ", 0, 4), ("ST", 0, 0), ("TY", 0, 1), ("NM", 0, 0),
    ("TZ", 1, 4), ("TZ", 1, 3), ("TY", 1, 0), ("TZ", 1, 2), ("M", 0, 0), ("TY", 0, 3), ("TY", 0, 2), ("A", 0, 0),
    ("M", 0, 1), ("A", 0, 1), ("TZ", 1, 1), ("B", 0, 0), ("M", 1, 0), ("TY", 1, 3), ("M", 0, 3), ("A", 1, 0),
    ("B", 0, 1), ("A", 0, 3), ("TY", 1, 1), ("TY", 1, 4), ("M", 0, 2), ("M", 1, 3), ("A", 0, 2), ("B", 1, 0),
    ("TY", 1, 2), ("B", 0, 3), ("C", 0, 0), ("A", 1, 3), ("TY", 0, 4), ("M", 1, 1), ("A", 1, 1), ("M", 1, 4),
    ("C", 1, 0), ("C", 0, 1), ("C", 0, 3), ("A", 1, 4), ("M", 1, 2), ("B", 1, 3), ("B", 0, 2), ("M", 0, 4),
    ("A", 0, 4), ("B", 1, 1), ("A", 1, 2), ("C", 0, 2), ("B", 0, 4), ("B", 1, 4), ("C", 1, 3), ("B", 1, 2),
    ("C", 1, 1), ("C", 0, 4), ("G", 0, 0), ("G", 0, 3), ("C", 1, 4), ("G", 0, 1), ("C", 1, 2), ("E1", 0, 0),
    ("E1", 1, 0), ("G", 0, 4), ("E1", 1, 1), ("G", 0, 2), ("E2", 1, 0), ("E2", 0, 0), ("E1", 1, 4), ("E1", 0, 3),
    ("E2", 1, 1), ("E1", 1, 3), ("E3", 1, 0), ("E1", 1, 2), ("F", 1, 0), ("E2", 0, 3), ("E3", 1, 1), ("E2", 1, 4),
    ("E3", 0, 0), ("E2", 1, 3), ("E1", 0, 1), ("F", 0, 0), ("E2", 1, 2), ("E3", 1, 4), ("E3", 0, 3), ("E1", 0, 4),
    ("H1", 1, 0), ("E1", 0, 2), ("F", 1, 4), ("F", 1, 1), ("F", 0, 3), ("E3", 1, 3), ("E3", 1, 2), ("E2", 0, 4),
    ("E2", 0, 1), ("F", 1, 3), ("H1", 0, 0), ("F", 1, 2), ("H", 1, 0), ("E2", 0, 2), ("E3", 0, 4), ("E3", 0, 1),
    ("H", 1, 1), ("F", 0, 4), ("H", 1, 4), ("H", 0, 3), ("H", 1, 3), ("H", 0, 0), ("E3", 0, 2), ("F", 0, 1),
    ("F", 0, 2), ("H", 1, 2), ("S", 0, 0), ("WD", 0, 0), ("WD", 0, 1), ("Z", 0, 0), ("H", 0, 1), ("H", 0, 4),
    ("H", 0, 2),
)


def transposed_dot(left, right):
    return lax.dot_general(left, right, (((1,), (1,)), ((), ())), preferred_element_type=F32)


def dot_transposed(left, right):
    return lax.dot_general(left, right, (((0,), (0,)), ((), ())), preferred_element_type=F32)


def columns_to_rows(first, second):
    lane = lax.broadcasted_iota(jnp.int32, (128, 128), 1)
    return jnp.where(lane == 0, first, jnp.where(lane == 1, second, 0.0)).T[0:8, :]


def rows_to_columns(first, second):
    row = lax.broadcasted_iota(jnp.int32, (128, 128), 0)
    both = jnp.where(row == 0, first, jnp.where(row == 1, second, 0.0)).T
    return both[:, 0:1], both[:, 1:2]


def column_sums(load, width):
    def block(i, total):
        return total + load(pl.ds(pl.multiple_of(i * 16, 16), 16)).astype(F32)

    return jnp.sum(lax.fori_loop(0, TOKENS // 16, block, jnp.zeros((16, width), F32)), axis=0)


def kernel(
    x_hbm, gain_hbm, bias_hbm, b_up_hbm, b_down_hbm, d_hbm, w_up_hbm, w_down_hbm,
    branch_hbm, grad_in_hbm, grad_gain_hbm, grad_bias_hbm, grad_b_up_hbm, grad_b_down_hbm, gw_down_hbm, gh_hbm, nrm_hbm,
    x_ref, gain_ref, bias_ref, b_up_ref, b_down_ref,
    branch_ref, grad_in_ref, grad_gain_ref, grad_bias_ref, grad_b_up_ref, grad_b_down_ref,
    w_up, w_down, dbr, nrm, part, core_in, x1_in, x2_in, z_in, full, t_out, t_in, t_acc,
    standard, grad_normed, inverse_ref, stats, back_stats, gb, b_up_sum,
    load_sem, store_sem, send_sem, recv_sem, small_send, small_recv,
):
    dp, tensor = lax.axis_index("dp"), lax.axis_index("tensor")
    xi, zh, core = dp // 4, (dp // 2) % 2, dp % 2
    yi, zl = tensor // 2, tensor % 2
    x_right, x_left, x_far = (xi + 1) % 4, (xi + 3) % 4, (xi + 2) % 4
    right = (x_right * 4 + zh * 2 + core, tensor)
    left = (x_left * 4 + zh * 2 + core, tensor)
    across = (xi * 4 + (1 - zh) * 2 + core, tensor)
    sibling = (xi * 4 + zh * 2 + (1 - core), tensor)
    t_pair = (dp, yi * 2 + (1 - zl))
    y_to = [(dp, ((yi + dy) % 4) * 2 + zl) for dy in (1, 2, 3)]
    t_to = y_to + [t_pair] + [(dp, ((yi + dy) % 4) * 2 + (1 - zl)) for dy in (1, 2, 3)]
    d_to = []
    for dx in range(4):
        for mz in range(2):
            for mc in range(2):
                if dx or mz or mc:
                    d_to.append((((xi + dx) % 4) * 4 + (1 - zh if mz else zh) * 2 + (1 - core if mc else core), tensor))

    barrier = pltpu.get_barrier_semaphore()
    for device in t_to + d_to:
        pl.semaphore_signal(barrier, inc=1, device_id=device, device_id_type=MESH)

    def rows_at(at, count):
        return pl.ds(pl.multiple_of(at, 16), count)

    pairs = [(d_hbm.at[pl.ds(OFF[c], OWN[c])], dbr.at[rows_at(8 * OFF[c] + tensor * OWN[c], OWN[c])]) for c in range(CHUNKS)]
    pairs += [(x_hbm, x_ref), (gain_hbm, gain_ref), (bias_hbm, bias_ref), (b_up_hbm, b_up_ref), (b_down_hbm, b_down_ref)]
    pairs += [(w_down_hbm, w_down)] + [(w_up_hbm.at[:, pl.ds(h * HALF, HALF)], w_up.at[h]) for h in range(2)]
    loads = [pltpu.make_async_copy(source, target, load_sem.at[i]) for i, (source, target) in enumerate(pairs)]
    for copy in loads:
        copy.start()
    loads = {"d": loads[:CHUNKS], "x": loads[CHUNKS : CHUNKS + 5], 0: loads[CHUNKS + 5 : CHUNKS + 6], 1: loads[CHUNKS + 6 :]}

    def loaded(name):
        for copy in loads.pop(name, ()):
            copy.wait()

    loaded("d")
    pl.semaphore_wait(barrier, len(t_to) + len(d_to))

    kinds = ("t", "tz", "core", "x1", "x2", "z", "ga", "gx", "gf", "gc", "ts", "tr")
    narrow = ("t", "tz", "ts", "tr")
    arriving, leaving = {}, {}

    def send(kind, k, c, source, target, device, rows):
        pltpu.make_async_remote_copy(
            src_ref=source, dst_ref=target, send_sem=send_sem.at[kinds.index(kind), k],
            recv_sem=recv_sem.at[kinds.index(kind), k, c], device_id=device, device_id_type=MESH,
        ).start()
        arriving[kind, k, c] = arriving.get((kind, k, c), 0) + rows
        leaving[kind, k] = leaving.get((kind, k), 0) + rows

    def wait_rows(kind, rows, semaphore):
        place = nrm.at[pl.ds(0, rows)] if kind in narrow else full.at[0, 0, pl.ds(0, rows)]
        pltpu.make_async_copy(place, place, semaphore).wait()

    def arrived(kind, k, c):
        wait_rows(kind, arriving.pop((kind, k, c)), recv_sem.at[kinds.index(kind), k, c])

    def send_small(index, buffer, devices):
        for s, device in enumerate(devices):
            pltpu.make_async_remote_copy(
                src_ref=buffer.at[0], dst_ref=buffer.at[s + 1], send_sem=small_send.at[index],
                recv_sem=small_recv.at[index], device_id=device, device_id_type=MESH,
            ).start()

    def wait_small(semaphore, buffer):
        place = buffer.at[pl.ds(1, buffer.shape[0] - 1)]
        pltpu.make_async_copy(place, place, semaphore).wait()

    stores = []

    def store(source, target):
        copy = pltpu.make_async_copy(source, target, store_sem.at[len(stores)])
        copy.start()
        stores.append(copy)

    tokens = (dbr, nrm)

    def pair_tokens(k, c):
        place = tokens[k].at[rows_at(8 * OFF[c] + tensor * OWN[c], OWN[c])]
        send("tz", k, c, place, place, t_pair, OWN[c])

    def gather_tokens(k, c):
        p = OWN[c]
        if c in T_PAIRS:
            arrived("tz", k, c)
            place = tokens[k].at[rows_at(8 * OFF[c] + yi * 2 * p, 2 * p)]
            for device in y_to:
                send("t", k, c, place, place, device, 2 * p)
        else:
            place = tokens[k].at[rows_at(8 * OFF[c] + tensor * p, p)]
            for device in t_to:
                send("t", k, c, place, place, device, p)

    def statistics(k, c):
        loaded("x")
        widened = x_ref[...].astype(F32)
        total = jnp.sum(widened, axis=1, keepdims=True)
        off = widened - total / WIDE
        stats[0] = columns_to_rows(total, jnp.sum(off * off, axis=1, keepdims=True))
        send_small(0, stats, d_to)

    def normalise(k, c):
        wait_small(small_recv.at[0], stats)
        sums = [stats[s, 0:1, :] for s in range(16)]
        mean = functools.reduce(jnp.add, sums) / D
        spread = jnp.zeros_like(mean)
        for s in range(16):
            apart = sums[s] / WIDE - mean
            spread = spread + (stats[s, 1:2, :] + WIDE * (apart * apart))
        mean, inverse = rows_to_columns(mean, lax.rsqrt(spread / D + 1e-05))
        inverse_ref[...] = jnp.broadcast_to(inverse, (128, 128))
        gain, bias = gain_ref[...].reshape(1, WIDE), bias_ref[...].reshape(1, WIDE)
        for c in range(CHUNKS):
            rows = slice(OFF[c], OFF[c] + OWN[c])
            std = (x_ref[rows, :].astype(F32) - mean[rows]) * inverse[rows]
            standard[rows, :] = std
            nrm[rows_at(8 * OFF[c] + tensor * OWN[c], OWN[c]), :] = (std * gain + bias).astype(BF16)

    def accumulate(k, c, start, count, others, columns=slice(None)):
        size = 32 if count % 32 == 0 else 16

        def block(i, _):
            at = i * size
            rows = rows_at(8 * OFF[c] + start + at, size)
            value = part[k, core, rows, columns].astype(F32)
            for load in others:
                value = value + load(at, size).astype(F32)
            part[k, core, rows, columns] = value.astype(BF16)
            return 0

        if count == size:
            block(0, 0)
        else:
            lax.fori_loop(0, count // size, block, 0)

    def multiply(k, c):
        loaded(k)
        arrived("t", k, c)
        rows = pl.ds(8 * OFF[c], 8 * OWN[c])

        def one(step, _):
            half = (1 - core) * (1 - step) + core * step
            if k:
                value = jnp.dot(nrm[rows, :], w_up[half], preferred_element_type=F32)
            else:
                value = transposed_dot(dbr[rows, :], w_down[half])
            part[k, half, rows, :] = value.astype(BF16)

            @pl.when(step == 0)
            def _():
                send("core", k, c, part.at[k, 1 - core, rows], core_in.at[k, rows], sibling, 8 * OWN[c])

            return 0

        lax.fori_loop(0, 2, one, 0)

    def part_rows(k, c, start, count):
        return part.at[k, core, rows_at(8 * OFF[c] + start, count)]

    def half_columns(side):
        return pl.ds(side * WIDE, WIDE)

    def add_core(k, c):
        p = OWN[c]
        arrived("core", k, c)

        def add(start, count):
            accumulate(k, c, start, count, [lambda at, size: core_in[k, rows_at(8 * OFF[c] + start + at, size), :]])

        if (k, c) in SUM_Z:
            for x in range(4):
                start = (2 * x + 1 - zh) * p
                add(start, p)
                send("z", k, c, part_rows(k, c, start, p), z_in.at[k, pl.ds(Z_OFF[k][c] + x * p, p)], across, p)
            for x in range(4):
                add((2 * x + zh) * p, p)
        else:
            add(x_far * 2 * p, 2 * p)
            for side, device in enumerate((right, left)):
                source = part_rows(k, c, x_far * 2 * p + side * p, p)
                send("x1", k, c, source, x1_in.at[k, side, pl.ds(OFF[c], p)], device, p)
            for piece in (x_right, x_left, xi):
                add(piece * 2 * p, 2 * p)

    def add_first(k, c):
        p = OWN[c]
        sides = ((x_right, right), (x_left, left))
        if (k, c) in SUM_Z:
            arrived("z", k, c)

            def add(piece):
                accumulate(
                    k, c, (2 * piece + zh) * p, p, [lambda at, size: z_in[k, rows_at(Z_OFF[k][c] + piece * p + at, size), :]]
                )

            add(x_far)
            far = part_rows(k, c, (2 * x_far + zh) * p, p)
            for side, (_, device) in enumerate(sides):
                target = x1_in.at[k, side, pl.ds(OFF[c], p), half_columns(side)]
                send("x1", k, c, far.at[:, half_columns(side)], target, device, p // 2)
            for piece in (x_right, x_left, xi):
                add(piece)
        else:
            arrived("x1", k, c)
            for side, (piece, device) in enumerate(sides):
                accumulate(
                    k, c, piece * 2 * p + side * p, p, [lambda at, size: x1_in[k, side, rows_at(OFF[c] + at, size), :]]
                )
                source = part_rows(k, c, piece * 2 * p, 2 * p)
                send("x2", k, c, source, x2_in.at[k, side, pl.ds(2 * OFF[c], 2 * p)], device, 2 * p)

    def add_second(k, c):
        p = OWN[c]
        if (k, c) in SUM_Z:
            arrived("x1", k, c)
            for side, (piece, device) in enumerate(((x_right, right), (x_left, left))):
                columns = half_columns(side)
                accumulate(
                    k, c, (2 * piece + zh) * p, p, [lambda at, size: x1_in[k, side, rows_at(OFF[c] + at, size), columns]], columns
                )
                source = part_rows(k, c, (2 * piece + zh) * p, p)
                send("x2", k, c, source, x2_in.at[k, side, pl.ds(2 * OFF[c], p)], device, p)
            return
        arrived("x2", k, c)

        def add(sub):
            start = sub * p
            accumulate(
                k, c, xi * 2 * p + start, p,
                [lambda at, size, side=side: x2_in[k, side, rows_at(2 * OFF[c] + start + at, size), :] for side in range(2)],
            )

        add(1 - zh)
        source = part_rows(k, c, xi * 2 * p + (1 - zh) * p, p)
        send("z", k, c, source, z_in.at[k, pl.ds(Z_OFF[k][c], p)], across, p)
        add(zh)

    def activate(_, c):
        p = OWN[c]
        mine = (2 * xi + zh) * p
        for k in range(2):
            arrived("x2" if (k, c) in SUM_Z else "z", k, c)
        bias = b_up_ref[pl.ds(pl.multiple_of(core * HALF, HALF), HALF)].reshape(1, HALF)

        def total(k, at):
            value = part[k, core, rows_at(8 * OFF[c] + mine + at, 16), :].astype(F32)
            if (k, c) in SUM_Z:
                for side in range(2):
                    value = value + x2_in[k, side, rows_at(2 * OFF[c] + at, 16), :].astype(F32)
                return value
            return value + z_in[k, rows_at(Z_OFF[k][c] + at, 16), :].astype(F32)

        def block(i, _):
            at = i * 16
            rows = rows_at(8 * OFF[c] + mine + at, 16)
            h = total(1, at) + bias
            square = h * h
            t = jnp.tanh(K0 * (h + K1 * (square * h)))
            full[0, core, rows, :] = (0.5 * h * (1.0 + t)).astype(BF16)
            slope = 0.5 * (1.0 + t) + 0.5 * h * (1.0 - t * t) * (K0 * (1.0 + 3.0 * K1 * square))
            full[1, core, rows, :] = (total(0, at) * slope).astype(BF16)
            return 0

        lax.fori_loop(0, p // 16, block, 0)
        for k in (1, 0):
            place = full.at[k, core, rows_at(8 * OFF[c] + mine, p)]
            for device in (right, left) if (k, c) in GATHER_X else (across,):
                send("ga", k, c, place, place, device, p)

    def full_rows(k, c, start, count):
        return full.at[k, core, rows_at(8 * OFF[c] + start, count)]

    def pass_on(kind, k, c, start, count, device):
        place = full_rows(k, c, start, count)
        send(kind, k, c, place, place, device, count)

    def gather_first(k, c):
        p = OWN[c]
        arrived("ga", k, c)
        if (k, c) in GATHER_X:
            for side, (piece, device) in enumerate(((x_left, right), (x_right, left))):
                place = full_rows(k, c, (2 * piece + zh) * p, p).at[:, half_columns(side)]
                send("gf", k, c, place, place, device, p // 2)
        else:
            for device in (right, left):
                pass_on("gx", k, c, xi * 2 * p, 2 * p, device)
            pass_on("gc", k, c, xi * 2 * p, 2 * p, sibling)

    def gather_second(k, c):
        p = OWN[c]
        if (k, c) in GATHER_X:
            arrived("gf", k, c)
            for x in range(4):
                pass_on("gx", k, c, (2 * x + zh) * p, p, across)
            for x in range(4):
                pass_on("gc", k, c, (2 * x + zh) * p, p, sibling)
        else:
            arrived("gx", k, c)
            for side, (piece, device) in enumerate(((x_left, right), (x_right, left))):
                pass_on("gf", k, c, piece * 2 * p + side * p, p, device)
            for piece in (x_left, x_right):
                pass_on("gc", k, c, piece * 2 * p, 2 * p, sibling)

    def gather_third(k, c):
        p = OWN[c]
        if (k, c) in GATHER_X:
            arrived("gx", k, c)
            for x in range(4):
                pass_on("gc", k, c, (2 * x + 1 - zh) * p, p, sibling)
        else:
            arrived("gf", k, c)
            pass_on("gc", k, c, x_far * 2 * p, 2 * p, sibling)

    def multiply_back(k, c):
        p = OWN[c]
        arrived("gc", k, c)
        rows = pl.ds(8 * OFF[c], 8 * p)

        def tile(j, _):
            at = pl.ds(pl.multiple_of(j * 256, 256), 256)
            if k:
                value = transposed_dot(full[1, 0, rows, :], w_up[0, at, :])
                value += transposed_dot(full[1, 1, rows, :], w_up[1, at, :])
            else:
                value = jnp.dot(full[0, 0, rows, :], w_down[0, :, at], preferred_element_type=F32)
                value += jnp.dot(full[0, 1, rows, :], w_down[1, :, at], preferred_element_type=F32)
            t_out[k, rows, at] = value.astype(BF16)
            return 0

        lax.fori_loop(0, WIDE // 256, tile, 0)
        if k:
            for half in range(2):
                store(full.at[1, half, rows], gh_hbm.at[rows, pl.ds(half * HALF, HALF)])
            store(nrm.at[rows], nrm_hbm.at[rows])
        if c in R_PAIRS:
            for s, device in enumerate(y_to):
                place = t_out.at[k, rows_at(8 * OFF[c] + (device[1] // 2) * 2 * p, 2 * p)]
                send("ts", k, c, place, t_in.at[k, pl.ds(7 * OFF[c] + s * 2 * p, 2 * p)], device, 2 * p)
        else:
            for s, device in enumerate(t_to):
                place = t_out.at[k, rows_at(8 * OFF[c] + device[1] * p, p)]
                send("ts", k, c, place, t_in.at[k, pl.ds(7 * OFF[c] + s * p, p)], device, p)
        if k:
            for half in range(2):

                def block(i, total):
                    return total + full[1, half, pl.ds(pl.multiple_of(8 * OFF[c] + i * 16, 16), 16), :].astype(F32)

                b_up_sum[half] = lax.fori_loop(0, p // 2, block, b_up_sum[half])

    def halve_tokens(k, c):
        p = OWN[c]
        arrived("ts", k, c)

        def total(sub):
            value = t_out[k, rows_at(8 * OFF[c] + (yi * 2 + sub) * p, p), :].astype(F32)
            for s in range(3):
                value = value + t_in[k, rows_at(7 * OFF[c] + s * 2 * p + sub * p, p), :].astype(F32)
            return value

        place = rows_at(8 * OFF[c] + (yi * 2 + 1 - zl) * p, p)
        t_out[k, place, :] = total(1 - zl).astype(BF16)
        send("tr", k, c, t_out.at[k, place], t_in.at[k, pl.ds(7 * OFF[c] + 6 * p, p)], t_pair, p)
        t_acc[k, OFF[c] : OFF[c] + p, :] = total(zl)

    def finish_tokens(k, c):
        p = OWN[c]
        rows = slice(OFF[c], OFF[c] + p)
        if c in R_PAIRS:
            arrived("tr", k, c)
            value = t_acc[k, rows, :] + t_in[k, 7 * OFF[c] + 6 * p : 7 * OFF[c] + 7 * p, :].astype(F32)
        else:
            arrived("ts", k, c)
            value = t_out[k, rows_at(8 * OFF[c] + tensor * p, p), :].astype(F32)
            for s in range(7):
                value = value + t_in[k, 7 * OFF[c] + s * p : 7 * OFF[c] + (s + 1) * p, :].astype(F32)
        if k:
            grad_normed[rows, :] = value
        else:
            branch_ref[rows, :] = (value + b_down_ref[...].reshape(1, WIDE)).astype(BF16)

    def weight_down(_, half):
        def strip(i, _):
            at = pl.ds(pl.multiple_of(i * STRIP, STRIP), STRIP)
            w_down[half, at, :] = dot_transposed(full[0, half, :, at], dbr[...]).astype(BF16)
            return 0

        lax.fori_loop(0, HALF // STRIP, strip, 0)
        store(w_down.at[half], gw_down_hbm.at[pl.ds(half * HALF, HALF)])
        if half == 0:
            grad_b_down_ref[...] = column_sums(lambda rows: dbr[rows, :], WIDE)

    def back_sums(k, c):
        gn, std = grad_normed[...], standard[...]
        scaled = gn * gain_ref[...].reshape(1, WIDE)
        back_stats[0] = columns_to_rows(
            jnp.sum(scaled, axis=1, keepdims=True), jnp.sum(scaled * std, axis=1, keepdims=True)
        )
        send_small(1, back_stats, d_to)
        gb[0, 0:1, :] = jnp.sum(gn * std, axis=0, keepdims=True)
        gb[0, 1:2, :] = jnp.sum(gn, axis=0, keepdims=True)
        gb[0, 2:8, :] = jnp.zeros((6, WIDE), F32)
        send_small(2, gb, t_to)

    def grad_inputs(k, c):
        wait_small(small_recv.at[1], back_stats)
        first = functools.reduce(jnp.add, [back_stats[s, 0:1, :] for s in range(16)]) / D
        second = functools.reduce(jnp.add, [back_stats[s, 1:2, :] for s in range(16)]) / D
        first, second = rows_to_columns(first, second)
        scaled = grad_normed[...] * gain_ref[...].reshape(1, WIDE)
        grad_in_ref[...] = (inverse_ref[:, 0:1] * (scaled - first - standard[...] * second)).astype(BF16)
        wait_small(small_recv.at[2], gb)
        both = functools.reduce(jnp.add, [gb[s] for s in range(8)])
        grad_gain_ref[...] = both[0]
        grad_bias_ref[...] = both[1]
        for half in range(2):
            grad_b_up_ref[half * HALF : (half + 1) * HALF] = jnp.sum(b_up_sum[half], axis=0)

    steps = {
        "TZ": pair_tokens, "TY": gather_tokens, "ST": statistics, "NM": normalise, "M": multiply, "A": add_core,
        "B": add_first, "C": add_second, "G": activate, "E1": gather_first, "E2": gather_second, "E3": gather_third,
        "F": multiply_back, "H1": halve_tokens, "H": finish_tokens, "WD": weight_down,
        "S": back_sums, "Z": grad_inputs,
    }
    b_up_sum[...] = jnp.zeros_like(b_up_sum)
    for name, k, c in ORDER:
        steps[name](k, c)
    for source, target in (
        (branch_ref, branch_hbm), (grad_in_ref, grad_in_hbm), (grad_gain_ref, grad_gain_hbm), (grad_bias_ref, grad_bias_hbm),
        (grad_b_up_ref, grad_b_up_hbm), (grad_b_down_ref, grad_b_down_hbm),
    ):
        store(source, target)
    for (kind, k), rows in leaving.items():
        wait_rows(kind, rows, send_sem.at[kinds.index(kind), k])
    for index, buffer in enumerate((stats, back_stats, gb)):
        wait_small(small_send.at[index], buffer)
    for copy in stores:
        copy.wait()


def last_kernel(
    nrm_hbm, gh_hbm, gw_down_hbm, branch_in, grad_in_in, gain_in, bias_in, b_up_in, b_down_in,
    branch_out, grad_in_out, gw_up_out, b_up_out, gw_down_out, b_down_out, gain_out, bias_out,
    nrm, gh, gw_up, gw_down, branch, grad_in, gain, bias, b_up, b_down, in_sem, out_sem,
):
    strips, parts = 2 * HALF // STRIP, 4

    def columns(i):
        return pl.ds(i * STRIP, STRIP)

    ins, outs = [], []

    def fetch(source, target):
        copy = pltpu.make_async_copy(source, target, in_sem.at[len(ins)])
        copy.start()
        ins.append(copy)
        return copy

    def put(source, target):
        copy = pltpu.make_async_copy(source, target, out_sem.at[len(outs)])
        copy.start()
        outs.append(copy)

    first = fetch(nrm_hbm, nrm)
    strip_in = [fetch(gh_hbm.at[:, columns(i)], gh.at[i]) for i in range(strips)]
    rows = [pl.ds(i * (2 * HALF // parts), 2 * HALF // parts) for i in range(parts)]
    passing = [(fetch(gw_down_hbm.at[r], gw_down.at[r]), gw_down.at[r], gw_down_out.at[r]) for r in rows]
    for source, held, target in (
        (branch_in, branch, branch_out), (grad_in_in, grad_in, grad_in_out), (gain_in, gain, gain_out),
        (bias_in, bias, bias_out), (b_up_in, b_up, b_up_out), (b_down_in, b_down, b_down_out),
    ):
        passing.append((fetch(source, held), held, target))
    first.wait()
    for i in range(strips):
        strip_in[i].wait()
        gw_up[i] = dot_transposed(nrm[...], gh[i]).astype(BF16)
        put(gw_up.at[i], gw_up_out.at[:, columns(i)])
        if i >= 2:
            for copy, held, target in passing[(i - 2) * 3 : (i - 1) * 3]:
                copy.wait()
                put(held, target)
    for copy in outs:
        copy.wait()


def on_device(inputs, norm_gain, norm_bias, w_up, b_up, w_down, b_down, d_branch):
    hbm = pl.BlockSpec(memory_space=pl.ANY)
    shape = jax.ShapeDtypeStruct

    dma = pltpu.SemaphoreType.DMA

    branch, grad_in, grad_gain, grad_bias, grad_b_up, grad_b_down, grad_w_down, gh, nrm = pl.pallas_call(
        kernel,
        out_shape=(
            shape((128, WIDE), BF16), shape((128, WIDE), BF16), shape((WIDE,), F32), shape((WIDE,), F32), shape((2 * HALF,), F32),
            shape((WIDE,), F32), shape((2 * HALF, WIDE), BF16), shape((TOKENS, 2 * HALF), BF16), shape((TOKENS, WIDE), BF16),
        ),
        in_specs=[hbm] * 8,
        out_specs=(hbm,) * 9,
        scratch_shapes=[
            pltpu.VMEM((128, WIDE), BF16),
            pltpu.VMEM((WIDE,), F32), pltpu.VMEM((WIDE,), F32), pltpu.VMEM((2 * HALF,), F32), pltpu.VMEM((WIDE,), F32),
            pltpu.VMEM((128, WIDE), BF16), pltpu.VMEM((128, WIDE), BF16),
            pltpu.VMEM((WIDE,), F32), pltpu.VMEM((WIDE,), F32), pltpu.VMEM((2 * HALF,), F32), pltpu.VMEM((WIDE,), F32),
            pltpu.VMEM((2, WIDE, HALF), BF16),
            pltpu.VMEM((2, HALF, WIDE), BF16),
            pltpu.VMEM((TOKENS, WIDE), BF16),
            pltpu.VMEM((TOKENS, WIDE), BF16),
            pltpu.VMEM((2, 2, TOKENS, HALF), BF16),
            pltpu.VMEM((2, TOKENS, HALF), BF16),
            pltpu.VMEM((2, 2, 128, HALF), BF16),
            pltpu.VMEM((2, 2, 256, HALF), BF16),
            pltpu.VMEM((2, max(sum(rows) for rows in Z_ROWS), HALF), BF16),
            pltpu.VMEM((2, 2, TOKENS, HALF), BF16),
            pltpu.VMEM((2, TOKENS, WIDE), BF16),
            pltpu.VMEM((2, 7 * 128, WIDE), BF16),
            pltpu.VMEM((2, 128, WIDE), F32),
            pltpu.VMEM((128, WIDE), F32),
            pltpu.VMEM((128, WIDE), F32),
            pltpu.VMEM((128, 128), F32),
            pltpu.VMEM((16, 8, 128), F32),
            pltpu.VMEM((16, 8, 128), F32),
            pltpu.VMEM((8, 8, WIDE), F32),
            pltpu.VMEM((2, 16, HALF), F32),
            dma((CHUNKS + 8,)), dma((8 + 3 * CHUNKS,)), dma((12, 2)), dma((12, 2, CHUNKS)), dma((3,)), dma((3,)),
        ],
        compiler_params=pltpu.CompilerParams(collective_id=0, has_side_effects=True, vmem_limit_bytes=63 * 2**20),
    )(inputs, norm_gain, norm_bias, b_up, b_down, d_branch, w_up, w_down.reshape(2, HALF, WIDE))
    return pl.pallas_call(
        last_kernel,
        out_shape=(
            shape((128, WIDE), BF16), shape((128, WIDE), BF16), shape((WIDE, 2 * HALF), BF16), shape((2 * HALF,), F32),
            shape((2 * HALF, WIDE), BF16), shape((WIDE,), F32), shape((WIDE,), F32), shape((WIDE,), F32),
        ),
        in_specs=[hbm] * 9,
        out_specs=(hbm,) * 8,
        scratch_shapes=[
            pltpu.VMEM((TOKENS, WIDE), BF16),
            pltpu.VMEM((6, TOKENS, STRIP), BF16),
            pltpu.VMEM((6, WIDE, STRIP), BF16),
            pltpu.VMEM((2 * HALF, WIDE), BF16),
            pltpu.VMEM((128, WIDE), BF16), pltpu.VMEM((128, WIDE), BF16),
            pltpu.VMEM((WIDE,), F32), pltpu.VMEM((WIDE,), F32), pltpu.VMEM((2 * HALF,), F32), pltpu.VMEM((WIDE,), F32),
            dma((17,)), dma((16,)),
        ],
        compiler_params=pltpu.CompilerParams(vmem_limit_bytes=63 * 2**20),
    )(nrm, gh, grad_w_down, branch, grad_in, grad_gain, grad_bias, grad_b_up, grad_b_down)


def solution(mesh):
    placed = (
        P("tensor", "dp"), P("dp"), P("dp"), P("dp", "tensor"), P("tensor"), P("tensor", "dp"), P("dp"), P("tensor", "dp"),
    )
    return jax.shard_map(
        on_device,
        mesh=mesh,
        in_specs=placed,
        out_specs=(
            P("tensor", "dp"), P("tensor", "dp"), P("dp", "tensor"), P("tensor"), P("tensor", "dp"), P("dp"), P("dp"), P("dp"),
        ),
        check_vma=False,
    )
```

time: 156 us -> 144 us (0.923)
  Pallas kernels: 155 us -> 143 us
    pallas_call x1, Pallas kernels: 143 us -> 134 us  [on_device(): pl.pallas_call(kernel, out_shape=(shape((128, WIDE), BF16), shape((128, W...]
    pallas_call x1, Pallas kernels: 11.9 us -> 8.98 us  [on_device(): pl.pallas_call(last_kernel, out_shape=(shape((128, WIDE), BF16), shape((1...]
where the time goes in v1:
time: 144 us
  Pallas kernels  143 us (99%)
    pallas_call x1, Pallas kernels, on_device(): pl.pallas_call(kernel, out_shape=(shape((128, WIDE), BF16), shape((128, W...  134 us
    pallas_call x1, Pallas kernels, on_device(): pl.pallas_call(last_kernel, out_shape=(shape((128, WIDE), BF16), shape((1...  8.98 us

profile of v1, /device:TPU:1, one launch (start us, length us, event | category | flops | bytes accessed | tf_op | source)
XLA Modules:
  0.0 143.8 jit_solution(11228955913526445816)
XLA Ops:
  0.6 134.0 %shard_map.143 = (bf16[128,768]{1,0:T(8,128)(2,1)}, bf16[128,768]{1,0:T(8,128)(2,1)}, f32[768]{0:T(1024)}, f32[768]{0:T(1024)}, f32[3072]{0:T(1024)}, /*index=5*...) custom-call(bf16[128,768]{1,0:T(8,128)(2,1)} %x_hbm.1, f32[768]{0:T(1024)} %gain_hbm.1, ...), custom_call_target="tpu_custom_call" | custom-call | tf_op jit(solution)/shard_map/pallas_call | solution.py:579
  134.7 9.0 %shard_map.144 = (bf16[128,768]{1,0:T(8,128)(2,1)}, bf16[128,768]{1,0:T(8,128)(2,1)}, bf16[768,3072]{1,0:T(8,128)(2,1)}, f32[3072]{0:T(1024)}, bf16[3072,768]{1,...) custom-call(bf16[1024,768]{1,0:T(8,128)(2,1)} %get-tuple-element.17.nrm_hbm, ...), custom_call_target="tpu_custom_call" | custom-call | tf_op jit(solution)/shard_map/pallas_call | solution.py:616

commit v2 on v1

--- a/solution.py
+++ b/solution.py
@@ -18,33 +18,36 @@
 K0 = 0.7978845608028654
 K1 = 0.044715
 
-OWN = (32, 32, 32, 16, 16)
+OWN = (32, 32, 16, 16, 16, 16)
 CHUNKS = len(OWN)
 OFF = tuple(sum(OWN[:c]) for c in range(CHUNKS))
-SUM_Z = ((0, 2), (0, 3), (1, 2))
-GATHER_X = ((0, 0), (0, 3), (1, 3))
-T_PAIRS = (1, 2, 3, 4)
-R_PAIRS = (0,)
+SUM_Z = ((0, 2), (0, 5), (1, 3), (1, 4), (1, 5))
+GATHER_X = ((0, 0), (0, 2), (1, 3), (1, 5))
+T_PAIRS = (1, 2, 3, 4, 5)
+R_PAIRS = (0, 2)
 Z_ROWS = tuple(tuple((4 if (k, c) in SUM_Z else 1) * OWN[c] for c in range(CHUNKS)) for k in range(2))
 Z_OFF = tuple(tuple(sum(rows[:c]) for c in range(CHUNKS)) for rows in Z_ROWS)
 
 ORDER = (
-    ("TZ", 0, 1), ("TY", 0, 0), ("TZ", 0, 3), ("TZ", 0, 2), ("TZ", 0, 4), ("ST", 0, 0), ("TY", 0, 1), ("NM", 0, 0),
-    ("TZ", 1, 4), ("TZ", 1, 3), ("TY", 1, 0), ("TZ", 1, 2), ("M", 0, 0), ("TY", 0, 3), ("TY", 0, 2), ("A", 0, 0),
-    ("M", 0, 1), ("A", 0, 1), ("TZ", 1, 1), ("B", 0, 0), ("M", 1, 0), ("TY", 1, 3), ("M", 0, 3), ("A", 1, 0),
-    ("B", 0, 1), ("A", 0, 3), ("TY", 1, 1), ("TY", 1, 4), ("M", 0, 2), ("M", 1, 3), ("A", 0, 2), ("B", 1, 0),
-    ("TY", 1, 2), ("B", 0, 3), ("C", 0, 0), ("A", 1, 3), ("TY", 0, 4), ("M", 1, 1), ("A", 1, 1), ("M", 1, 4),
-    ("C", 1, 0), ("C", 0, 1), ("C", 0, 3), ("A", 1, 4), ("M", 1, 2), ("B", 1, 3), ("B", 0, 2), ("M", 0, 4),
-    ("A", 0, 4), ("B", 1, 1), ("A", 1, 2), ("C", 0, 2), ("B", 0, 4), ("B", 1, 4), ("C", 1, 3), ("B", 1, 2),
-    ("C", 1, 1), ("C", 0, 4), ("G", 0, 0), ("G", 0, 3), ("C", 1, 4), ("G", 0, 1), ("C", 1, 2), ("E1", 0, 0),
-    ("E1", 1, 0), ("G", 0, 4), ("E1", 1, 1), ("G", 0, 2), ("E2", 1, 0), ("E2", 0, 0), ("E1", 1, 4), ("E1", 0, 3),
-    ("E2", 1, 1), ("E1", 1, 3), ("E3", 1, 0), ("E1", 1, 2), ("F", 1, 0), ("E2", 0, 3), ("E3", 1, 1), ("E2", 1, 4),
-    ("E3", 0, 0), ("E2", 1, 3), ("E1", 0, 1), ("F", 0, 0), ("E2", 1, 2), ("E3", 1, 4), ("E3", 0, 3), ("E1", 0, 4),
-    ("H1", 1, 0), ("E1", 0, 2), ("F", 1, 4), ("F", 1, 1), ("F", 0, 3), ("E3", 1, 3), ("E3", 1, 2), ("E2", 0, 4),
-    ("E2", 0, 1), ("F", 1, 3), ("H1", 0, 0), ("F", 1, 2), ("H", 1, 0), ("E2", 0, 2), ("E3", 0, 4), ("E3", 0, 1),
-    ("H", 1, 1), ("F", 0, 4), ("H", 1, 4), ("H", 0, 3), ("H", 1, 3), ("H", 0, 0), ("E3", 0, 2), ("F", 0, 1),
-    ("F", 0, 2), ("H", 1, 2), ("S", 0, 0), ("WD", 0, 0), ("WD", 0, 1), ("Z", 0, 0), ("H", 0, 1), ("H", 0, 4),
-    ("H", 0, 2),
+    ("TZ", 0, 2), ("TZ", 0, 3), ("TY", 0, 0), ("ST", 0, 0), ("TZ", 0, 4), ("TZ", 0, 1), ("TY", 0, 2), ("NM", 0, 0),
+    ("TZ", 1, 3), ("TY", 0, 3), ("TZ", 1, 2), ("TZ", 0, 5), ("TZ", 1, 5), ("TZ", 1, 4), ("TY", 1, 0), ("M", 0, 0),
+    ("TY", 1, 3), ("TZ", 1, 1), ("TY", 1, 2), ("A", 0, 0), ("M", 0, 2), ("M", 0, 3), ("TY", 0, 5), ("B", 0, 0),
+    ("A", 0, 2), ("M", 1, 0), ("TY", 0, 1), ("TY", 1, 4), ("A", 0, 3), ("A", 1, 0), ("M", 1, 3), ("TY", 1, 5),
+    ("B", 0, 2), ("C", 0, 0), ("B", 0, 3), ("M", 0, 5), ("B", 1, 0), ("A", 1, 3), ("A", 0, 5), ("TY", 0, 4),
+    ("C", 0, 2), ("M", 1, 2), ("M", 0, 1), ("TY", 1, 1), ("A", 1, 2), ("A", 0, 1), ("M", 1, 5), ("B", 1, 3),
+    ("C", 1, 0), ("C", 0, 3), ("B", 1, 2), ("A", 1, 5), ("B", 0, 1), ("C", 1, 3), ("M", 1, 4), ("C", 1, 2),
+    ("M", 1, 1), ("G", 0, 0), ("A", 1, 4), ("A", 1, 1), ("B", 0, 5), ("C", 0, 1), ("M", 0, 4), ("E1", 0, 0),
+    ("B", 1, 5), ("A", 0, 4), ("B", 1, 1), ("C", 1, 5), ("G", 0, 3), ("E2", 0, 0), ("C", 0, 5), ("B", 1, 4),
+    ("E1", 1, 0), ("C", 1, 1), ("G", 0, 2), ("B", 0, 4), ("C", 1, 4), ("G", 0, 5), ("E3", 0, 0), ("G", 0, 1),
+    ("E1", 0, 2), ("E2", 1, 0), ("F", 0, 0), ("E1", 1, 2), ("C", 0, 4), ("E1", 0, 5), ("E1", 1, 3), ("E1", 1, 5),
+    ("E2", 0, 2), ("E3", 1, 0), ("E2", 1, 2), ("E1", 1, 1), ("G", 0, 4), ("F", 1, 0), ("E2", 1, 3), ("E3", 1, 2),
+    ("E3", 0, 2), ("E2", 1, 5), ("E2", 0, 5), ("E1", 1, 4), ("F", 1, 2), ("E1", 0, 3), ("F", 0, 2), ("E2", 1, 1),
+    ("E3", 0, 5), ("E1", 0, 4), ("E3", 1, 3), ("F", 0, 5), ("F", 1, 3), ("H1", 0, 0), ("E2", 1, 4), ("H1", 1, 0),
+    ("E3", 1, 5), ("H1", 1, 2), ("E3", 1, 1), ("E1", 0, 1), ("F", 1, 5), ("H1", 0, 2), ("F", 1, 1), ("E2", 0, 3),
+    ("E3", 1, 4), ("H", 1, 0), ("E2", 0, 4), ("E2", 0, 1), ("H", 1, 3), ("F", 1, 4), ("H", 0, 0), ("E3", 0, 3),
+    ("H", 0, 2), ("E3", 0, 4), ("H", 0, 5), ("H", 1, 2), ("H", 1, 5), ("F", 0, 3), ("E3", 0, 1), ("F", 0, 4),
+    ("F", 0, 1), ("WD", 0, 1), ("H", 1, 4), ("H", 1, 1), ("S", 0, 0), ("H", 0, 3), ("WD", 0, 0), ("Z", 0, 0),
+    ("H", 0, 1), ("H", 0, 4),
 )
 
 
@@ -65,13 +68,6 @@
     row = lax.broadcasted_iota(jnp.int32, (128, 128), 0)
     both = jnp.where(row == 0, first, jnp.where(row == 1, second, 0.0)).T
     return both[:, 0:1], both[:, 1:2]
-
-
-def column_sums(load, width):
-    def block(i, total):
-        return total + load(pl.ds(pl.multiple_of(i * 16, 16), 16)).astype(F32)
-
-    return jnp.sum(lax.fori_loop(0, TOKENS // 16, block, jnp.zeros((16, width), F32)), axis=0)
 
 
 def kernel(
@@ -80,8 +76,8 @@
     x_ref, gain_ref, bias_ref, b_up_ref, b_down_ref,
     branch_ref, grad_in_ref, grad_gain_ref, grad_bias_ref, grad_b_up_ref, grad_b_down_ref,
     w_up, w_down, dbr, nrm, part, core_in, x1_in, x2_in, z_in, full, t_out, t_in, t_acc,
-    standard, grad_normed, inverse_ref, stats, back_stats, gb, b_up_sum,
-    load_sem, store_sem, send_sem, recv_sem, small_send, small_recv,
+    standard, grad_normed, inverse_ref, stats, back_stats, gb, b_up_sum, b_down_sum,
+    load_sem, store_sem, strip_sem, send_sem, recv_sem, small_send, small_recv,
 ):
     dp, tensor = lax.axis_index("dp"), lax.axis_index("tensor")
     xi, zh, core = dp // 4, (dp // 2) % 2, dp % 2
@@ -240,6 +236,12 @@
             return 0
 
         lax.fori_loop(0, 2, one, 0)
+        if not k:
+
+            def block(i, total):
+                return total + dbr[pl.ds(pl.multiple_of(8 * OFF[c] + i * 16, 16), 16), :].astype(F32)
+
+            b_down_sum[...] = lax.fori_loop(0, OWN[c] // 2, block, b_down_sum[...])
 
     def part_rows(k, c, start, count):
         return part.at[k, core, rows_at(8 * OFF[c] + start, count)]
@@ -470,12 +472,11 @@
         def strip(i, _):
             at = pl.ds(pl.multiple_of(i * STRIP, STRIP), STRIP)
             w_down[half, at, :] = dot_transposed(full[0, half, :, at], dbr[...]).astype(BF16)
+            target = gw_down_hbm.at[pl.ds(pl.multiple_of(half * HALF + i * STRIP, STRIP), STRIP)]
+            pltpu.make_async_copy(w_down.at[half, at], target, strip_sem.at[half]).start()
             return 0
 
         lax.fori_loop(0, HALF // STRIP, strip, 0)
-        store(w_down.at[half], gw_down_hbm.at[pl.ds(half * HALF, HALF)])
-        if half == 0:
-            grad_b_down_ref[...] = column_sums(lambda rows: dbr[rows, :], WIDE)
 
     def back_sums(k, c):
         gn, std = grad_normed[...], standard[...]
@@ -488,6 +489,11 @@
         gb[0, 1:2, :] = jnp.sum(gn, axis=0, keepdims=True)
         gb[0, 2:8, :] = jnp.zeros((6, WIDE), F32)
         send_small(2, gb, t_to)
+        for half in range(2):
+            grad_b_up_ref[half * HALF : (half + 1) * HALF] = jnp.sum(b_up_sum[half], axis=0)
+        grad_b_down_ref[...] = jnp.sum(b_down_sum[...], axis=0)
+        store(grad_b_up_ref, grad_b_up_hbm)
+        store(grad_b_down_ref, grad_b_down_hbm)
 
     def grad_inputs(k, c):
         wait_small(small_recv.at[1], back_stats)
@@ -496,12 +502,13 @@
         first, second = rows_to_columns(first, second)
         scaled = grad_normed[...] * gain_ref[...].reshape(1, WIDE)
         grad_in_ref[...] = (inverse_ref[:, 0:1] * (scaled - first - standard[...] * second)).astype(BF16)
+        store(grad_in_ref, grad_in_hbm)
         wait_small(small_recv.at[2], gb)
         both = functools.reduce(jnp.add, [gb[s] for s in range(8)])
         grad_gain_ref[...] = both[0]
         grad_bias_ref[...] = both[1]
-        for half in range(2):
-            grad_b_up_ref[half * HALF : (half + 1) * HALF] = jnp.sum(b_up_sum[half], axis=0)
+        store(grad_gain_ref, grad_gain_hbm)
+        store(grad_bias_ref, grad_bias_hbm)
 
     steps = {
         "TZ": pair_tokens, "TY": gather_tokens, "ST": statistics, "NM": normalise, "M": multiply, "A": add_core,
@@ -510,19 +517,18 @@
         "S": back_sums, "Z": grad_inputs,
     }
     b_up_sum[...] = jnp.zeros_like(b_up_sum)
+    b_down_sum[...] = jnp.zeros_like(b_down_sum)
     for name, k, c in ORDER:
         steps[name](k, c)
-    for source, target in (
-        (branch_ref, branch_hbm), (grad_in_ref, grad_in_hbm), (grad_gain_ref, grad_gain_hbm), (grad_bias_ref, grad_bias_hbm),
-        (grad_b_up_ref, grad_b_up_hbm), (grad_b_down_ref, grad_b_down_hbm),
-    ):
-        store(source, target)
+    store(branch_ref, branch_hbm)
     for (kind, k), rows in leaving.items():
         wait_rows(kind, rows, send_sem.at[kinds.index(kind), k])
     for index, buffer in enumerate((stats, back_stats, gb)):
         wait_small(small_send.at[index], buffer)
     for copy in stores:
         copy.wait()
+    for half in range(2):
+        pltpu.make_async_copy(w_down.at[half], gw_down_hbm.at[pl.ds(half * HALF, HALF)], strip_sem.at[half]).wait()
 
 
 def last_kernel(
@@ -609,7 +615,8 @@
             pltpu.VMEM((16, 8, 128), F32),
             pltpu.VMEM((8, 8, WIDE), F32),
             pltpu.VMEM((2, 16, HALF), F32),
-            dma((CHUNKS + 8,)), dma((8 + 3 * CHUNKS,)), dma((12, 2)), dma((12, 2, CHUNKS)), dma((3,)), dma((3,)),
+            pltpu.VMEM((16, WIDE), F32),
+            dma((CHUNKS + 8,)), dma((6 + 3 * CHUNKS,)), dma((2,)), dma((12, 2)), dma((12, 2, CHUNKS)), dma((3,)), dma((3,)),
         ],
         compiler_params=pltpu.CompilerParams(collective_id=0, has_side_effects=True, vmem_limit_bytes=63 * 2**20),
     )(inputs, norm_gain, norm_bias, b_up, b_down, d_branch, w_up, w_down.reshape(2, HALF, WIDE))

time: 144 us -> 141 us (0.979)
  Pallas kernels: 143 us -> 140 us
    pallas_call x1, Pallas kernels: 134 us -> 131 us  [on_device(): pl.pallas_call(kernel, out_shape=(shape((128, WIDE), BF16), shape((128, W...]
where the time goes in v2:
time: 141 us
  Pallas kernels  140 us (99%)
    pallas_call x1, Pallas kernels, on_device(): pl.pallas_call(kernel, out_shape=(shape((128, WIDE), BF16), shape((128, W...  131 us
    pallas_call x1, Pallas kernels, on_device(): pl.pallas_call(last_kernel, out_shape=(shape((128, WIDE), BF16), shape((1...  8.98 us

profile of v2, /device:TPU:1, one launch (start us, length us, event | category | flops | bytes accessed | tf_op | source)
XLA Modules:
  0.0 140.6 jit_solution(7073687627431929914)
XLA Ops:
  0.6 130.9 %shard_map.143 = (bf16[128,768]{1,0:T(8,128)(2,1)}, bf16[128,768]{1,0:T(8,128)(2,1)}, f32[768]{0:T(1024)}, f32[768]{0:T(1024)}, f32[3072]{0:T(1024)}, /*index=5*...) custom-call(bf16[128,768]{1,0:T(8,128)(2,1)} %x_hbm.1, f32[768]{0:T(1024)} %gain_hbm.1, ...), custom_call_target="tpu_custom_call" | custom-call | tf_op jit(solution)/shard_map/pallas_call | solution.py:585
  131.5 9.0 %shard_map.144 = (bf16[128,768]{1,0:T(8,128)(2,1)}, bf16[128,768]{1,0:T(8,128)(2,1)}, bf16[768,3072]{1,0:T(8,128)(2,1)}, f32[3072]{0:T(1024)}, bf16[3072,768]{1,...) custom-call(bf16[1024,768]{1,0:T(8,128)(2,1)} %get-tuple-element.17.nrm_hbm, ...), custom_call_target="tpu_custom_call" | custom-call | tf_op jit(solution)/shard_map/pallas_call | solution.py:623

commit v3 on v2

--- a/solution.py
+++ b/solution.py
@@ -21,7 +21,7 @@
 OWN = (32, 32, 16, 16, 16, 16)
 CHUNKS = len(OWN)
 OFF = tuple(sum(OWN[:c]) for c in range(CHUNKS))
-SUM_Z = ((0, 2), (0, 5), (1, 3), (1, 4), (1, 5))
+SUM_Z = ((0, 3), (0, 5), (1, 3), (1, 4), (1, 5))
 GATHER_X = ((0, 0), (0, 2), (1, 3), (1, 5))
 T_PAIRS = (1, 2, 3, 4, 5)
 R_PAIRS = (0, 2)
@@ -29,25 +29,25 @@
 Z_OFF = tuple(tuple(sum(rows[:c]) for c in range(CHUNKS)) for rows in Z_ROWS)
 
 ORDER = (
-    ("TZ", 0, 2), ("TZ", 0, 3), ("TY", 0, 0), ("ST", 0, 0), ("TZ", 0, 4), ("TZ", 0, 1), ("TY", 0, 2), ("NM", 0, 0),
-    ("TZ", 1, 3), ("TY", 0, 3), ("TZ", 1, 2), ("TZ", 0, 5), ("TZ", 1, 5), ("TZ", 1, 4), ("TY", 1, 0), ("M", 0, 0),
-    ("TY", 1, 3), ("TZ", 1, 1), ("TY", 1, 2), ("A", 0, 0), ("M", 0, 2), ("M", 0, 3), ("TY", 0, 5), ("B", 0, 0),
-    ("A", 0, 2), ("M", 1, 0), ("TY", 0, 1), ("TY", 1, 4), ("A", 0, 3), ("A", 1, 0), ("M", 1, 3), ("TY", 1, 5),
-    ("B", 0, 2), ("C", 0, 0), ("B", 0, 3), ("M", 0, 5), ("B", 1, 0), ("A", 1, 3), ("A", 0, 5), ("TY", 0, 4),
-    ("C", 0, 2), ("M", 1, 2), ("M", 0, 1), ("TY", 1, 1), ("A", 1, 2), ("A", 0, 1), ("M", 1, 5), ("B", 1, 3),
-    ("C", 1, 0), ("C", 0, 3), ("B", 1, 2), ("A", 1, 5), ("B", 0, 1), ("C", 1, 3), ("M", 1, 4), ("C", 1, 2),
-    ("M", 1, 1), ("G", 0, 0), ("A", 1, 4), ("A", 1, 1), ("B", 0, 5), ("C", 0, 1), ("M", 0, 4), ("E1", 0, 0),
-    ("B", 1, 5), ("A", 0, 4), ("B", 1, 1), ("C", 1, 5), ("G", 0, 3), ("E2", 0, 0), ("C", 0, 5), ("B", 1, 4),
-    ("E1", 1, 0), ("C", 1, 1), ("G", 0, 2), ("B", 0, 4), ("C", 1, 4), ("G", 0, 5), ("E3", 0, 0), ("G", 0, 1),
-    ("E1", 0, 2), ("E2", 1, 0), ("F", 0, 0), ("E1", 1, 2), ("C", 0, 4), ("E1", 0, 5), ("E1", 1, 3), ("E1", 1, 5),
-    ("E2", 0, 2), ("E3", 1, 0), ("E2", 1, 2), ("E1", 1, 1), ("G", 0, 4), ("F", 1, 0), ("E2", 1, 3), ("E3", 1, 2),
-    ("E3", 0, 2), ("E2", 1, 5), ("E2", 0, 5), ("E1", 1, 4), ("F", 1, 2), ("E1", 0, 3), ("F", 0, 2), ("E2", 1, 1),
-    ("E3", 0, 5), ("E1", 0, 4), ("E3", 1, 3), ("F", 0, 5), ("F", 1, 3), ("H1", 0, 0), ("E2", 1, 4), ("H1", 1, 0),
-    ("E3", 1, 5), ("H1", 1, 2), ("E3", 1, 1), ("E1", 0, 1), ("F", 1, 5), ("H1", 0, 2), ("F", 1, 1), ("E2", 0, 3),
-    ("E3", 1, 4), ("H", 1, 0), ("E2", 0, 4), ("E2", 0, 1), ("H", 1, 3), ("F", 1, 4), ("H", 0, 0), ("E3", 0, 3),
-    ("H", 0, 2), ("E3", 0, 4), ("H", 0, 5), ("H", 1, 2), ("H", 1, 5), ("F", 0, 3), ("E3", 0, 1), ("F", 0, 4),
-    ("F", 0, 1), ("WD", 0, 1), ("H", 1, 4), ("H", 1, 1), ("S", 0, 0), ("H", 0, 3), ("WD", 0, 0), ("Z", 0, 0),
-    ("H", 0, 1), ("H", 0, 4),
+    ("TZ", 0, 3), ("TZ", 0, 2), ("TY", 0, 0), ("ST", 0, 0), ("TZ", 0, 1), ("TY", 0, 2), ("TY", 0, 3), ("NM", 0, 0),
+    ("TZ", 1, 3), ("TZ", 0, 5), ("TY", 1, 0), ("TZ", 1, 2), ("M", 0, 0), ("TZ", 1, 5), ("TZ", 1, 4), ("TZ", 1, 1),
+    ("TY", 1, 3), ("A", 0, 0), ("M", 0, 2), ("M", 0, 3), ("A", 0, 2), ("TY", 1, 2), ("TZ", 0, 4), ("B", 0, 0),
+    ("A", 0, 3), ("TY", 0, 5), ("TY", 0, 1), ("M", 1, 0), ("M", 1, 3), ("A", 1, 0), ("TY", 1, 5), ("B", 0, 2),
+    ("M", 1, 2), ("A", 1, 3), ("TY", 1, 4), ("TY", 1, 1), ("A", 1, 2), ("B", 0, 3), ("M", 0, 5), ("B", 1, 0),
+    ("A", 0, 5), ("TY", 0, 4), ("M", 0, 1), ("B", 1, 3), ("A", 0, 1), ("B", 1, 2), ("C", 0, 0), ("M", 1, 4),
+    ("M", 1, 5), ("C", 1, 0), ("C", 0, 3), ("A", 1, 4), ("B", 0, 1), ("M", 1, 1), ("A", 1, 5), ("G", 0, 0),
+    ("M", 0, 4), ("A", 1, 1), ("C", 1, 3), ("C", 0, 1), ("E1", 0, 0), ("A", 0, 4), ("B", 0, 5), ("B", 1, 5),
+    ("C", 1, 2), ("C", 0, 2), ("B", 1, 1), ("E2", 0, 0), ("C", 0, 5), ("E1", 1, 0), ("C", 1, 5), ("B", 0, 4),
+    ("C", 1, 1), ("B", 1, 4), ("G", 0, 2), ("G", 0, 3), ("G", 0, 5), ("C", 0, 4), ("C", 1, 4), ("E3", 0, 0),
+    ("E1", 0, 2), ("E2", 1, 0), ("G", 0, 1), ("E1", 1, 2), ("E1", 1, 3), ("E1", 0, 5), ("E2", 0, 2), ("E1", 1, 5),
+    ("F", 0, 0), ("E3", 1, 0), ("E2", 1, 2), ("E1", 1, 1), ("G", 0, 4), ("E2", 1, 3), ("F", 1, 0), ("E2", 0, 5),
+    ("E3", 0, 2), ("E3", 1, 2), ("E1", 1, 4), ("E1", 0, 4), ("E2", 1, 5), ("F", 0, 2), ("E2", 1, 1), ("F", 1, 2),
+    ("E3", 0, 5), ("H1", 0, 0), ("E3", 1, 3), ("F", 0, 5), ("E2", 1, 4), ("E1", 0, 3), ("F", 1, 3), ("H1", 0, 2),
+    ("E3", 1, 5), ("E3", 1, 1), ("E1", 0, 1), ("E2", 0, 4), ("H1", 1, 0), ("F", 1, 5), ("H1", 1, 2), ("F", 1, 1),
+    ("H", 1, 3), ("E3", 1, 4), ("H", 0, 5), ("E2", 0, 3), ("H", 1, 0), ("E2", 0, 1), ("H", 0, 0), ("F", 1, 4),
+    ("E3", 0, 3), ("H", 1, 2), ("E3", 0, 4), ("F", 0, 3), ("H", 0, 2), ("H", 1, 5), ("E3", 0, 1), ("F", 0, 4),
+    ("H", 1, 1), ("F", 0, 1), ("H", 1, 4), ("S", 0, 0), ("WD", 0, 1), ("WD", 0, 0), ("Z", 0, 0), ("H", 0, 4),
+    ("H", 0, 3), ("H", 0, 1),
 )
 
 

time: 141 us -> 139 us (0.986)
  Pallas kernels: 140 us -> 138 us
    pallas_call x1, Pallas kernels: 131 us -> 129 us  [on_device(): pl.pallas_call(kernel, out_shape=(shape((128, WIDE), BF16), shape((128, W...]
where the time goes in v3:
time: 139 us; the launch traced here: 138 us
  Pallas kernels  138 us (99%)
    pallas_call x1, Pallas kernels, on_device(): pl.pallas_call(kernel, out_shape=(shape((128, WIDE), BF16), shape((128, W...  129 us
    pallas_call x1, Pallas kernels, on_device(): pl.pallas_call(last_kernel, out_shape=(shape((128, WIDE), BF16), shape((1...  8.98 us

profile of v3, /device:TPU:1, one launch (start us, length us, event | category | flops | bytes accessed | tf_op | source)
XLA Modules:
  0.0 138.5 jit_solution(4182981583029373609)
XLA Ops:
  0.6 128.7 %shard_map.143 = (bf16[128,768]{1,0:T(8,128)(2,1)}, bf16[128,768]{1,0:T(8,128)(2,1)}, f32[768]{0:T(1024)}, f32[768]{0:T(1024)}, f32[3072]{0:T(1024)}, /*index=5*...) custom-call(bf16[128,768]{1,0:T(8,128)(2,1)} %x_hbm.1, f32[768]{0:T(1024)} %gain_hbm.1, ...), custom_call_target="tpu_custom_call" | custom-call | tf_op jit(solution)/shard_map/pallas_call | solution.py:585
  129.4 9.0 %shard_map.144 = (bf16[128,768]{1,0:T(8,128)(2,1)}, bf16[128,768]{1,0:T(8,128)(2,1)}, bf16[768,3072]{1,0:T(8,128)(2,1)}, f32[3072]{0:T(1024)}, bf16[3072,768]{1,...) custom-call(bf16[1024,768]{1,0:T(8,128)(2,1)} %get-tuple-element.17.nrm_hbm, ...), custom_call_target="tpu_custom_call" | custom-call | tf_op jit(solution)/shard_map/pallas_call | solution.py:623
